TPU v7x, 32 devices: a whole 2x2x4 slice. The times are simulated.
32 devices in a mesh: grp: 2 (over y), prow: 4 (over z), pcol: 4 (over x, core).
Axes of the slice: x: 2, y: 2, z: 4, core: 2. Of those that a mesh axis runs over, the one named last changes fastest.
Arguments:
- eigvecs: float32 [8192, 4096], P(('grp', 'prow'), 'pcol'), parts along dimension 0, may hold values from -6 to 6
- y_panels: float32 [2, 8192, 256], P(None, ('grp', 'prow'), 'pcol'), parts along dimension 1, as said below
- t_factors: float32 [4, 256, 256], P('grp'), parts along dimension 0, as said below
Outputs:
- result: float32 [8192, 4096], P(('grp', 'prow'), 'pcol'), parts along dimension 0
There are 2 independent parts, one for each index of `grp`. A program takes and returns all parts, laid end to end along the dimension named above; each array names one. Nothing has to cross between parts.
Inputs may be any that keep to these rules, and one draw needn't show every extreme that they name: `y_panels`: column j of panel k is zero in rows above k * 256 + j and one in that row; t_factors[k] is upper triangular with diagonal between 0.5 and 1.5. Each t_factors[k] is upper triangular.
All inputs are finite; a program needn't handle non-finite values.
Results may differ from a plain program's by a relative error of at most 0.0001.
Values sent between devices are 32-bit elements; how exact they have to be, the bound alone decides.
A program may use at most 64 MiB of HBM per device.

v0:
```python
import jax
import jax.numpy as jnp
from jax import lax
from jax.sharding import PartitionSpec as P


def update(current, vectors, triangle):
    highest = lax.Precision.HIGHEST
    local_sums = jnp.einsum("rc,rk->ck", current, vectors, precision=highest)
    sums = lax.psum(local_sums, "prow")
    scaled = jnp.einsum("ck,jk->cj", sums, triangle, precision=highest)
    return current - jnp.einsum("rj,cj->rc", vectors, scaled, precision=highest)


def per_device(eigvecs, y_panels, t_factors):
    gathered = lax.all_gather(y_panels, "pcol", axis=2, tiled=True)
    count = gathered.shape[0]
    current = eigvecs
    for index in reversed(range(count)):
        current = update(current, gathered[index], t_factors[index])
    return current


def solution(mesh):
    return jax.shard_map(
        per_device,
        mesh=mesh,
        in_specs=(
            P(("grp", "prow"), "pcol"),
            P(None, ("grp", "prow"), "pcol"),
            P("grp", None, None),
        ),
        out_specs=P(("grp", "prow"), "pcol"),
        check_vma=False,
    )
```

profile of v0, /device:TPU:0, one launch (start us, length us, event | category | flops | bytes accessed | tf_op | source)
XLA Modules:
  0.0 183.0 jit_solution(13575742015813939483)
XLA Ops:
  6.5 0.0 all-gather.2.cloned.1.call-start
  6.5 0.7 all-gather.2.cloned.1.call-update
  7.3 0.0 all-reduce.3.cloned.1.call-start
  7.3 26.9 %all-gather.2.cloned.1.call-done = f32[2,1024,256]{1,2,0:T(8,128)} async-done(((f32[2,1024,64]{1,2,0:T(8,128)}), f32[2,1024,256]{1,2,0:T(8,128)}) %all-gather.2.cloned.1.call-update) | async-done | bytes 2097168 | tf_op jit(solution)/shard_map/all_gather | solution.py:16
  34.2 10.1 %fusion = f32[1024,256]{1,0:T(8,128)} fusion(f32[1024,1024]{1,0:T(8,128)} %param.3, f32[2,1024,256]{1,2,0:T(8,128)} %all-gather.2.cloned.1.call-done), kind=kOutput, calls=%fused_computation.4 | convolution fusion | flops 3221225472 | bytes 6291456 | tf_op jit(solution)/shard_map/rc,rk->ck/dot_general | solution.py:9
  44.4 0.0 all-reduce.3.cloned.1.call-update
  44.4 0.0 copy-start.2
  44.4 0.0 copy-start.1
  44.4 0.2 all-reduce.5.cloned.1.call-start
  44.7 5.5 %copy.4 = f32[1024,1024]{0,1:T(8,128)} copy(f32[1024,1024]{1,0:T(8,128)} %param.3) | data formatting | bytes 8388608 | tf_op args[0]
  50.1 46.3 %all-reduce.3.cloned.1.call-done = f32[1024,256]{1,0:T(8,128)} async-done(((f32[1024,256]{1,0:T(8,128)}), f32[1024,256]{1,0:T(8,128)}) %all-reduce.3.cloned.1.call-update) | async-done | bytes 1048592 | tf_op jit(solution)/shard_map/psum | solution.py:10
  96.4 0.0 copy-done.2
  96.4 2.3 %fusion.4 = f32[1024,256]{1,0:T(8,128)S(1)} fusion(f32[1024,256]{1,0:T(8,128)} %all-reduce.3.cloned.1.call-done, f32[2,256,256]{2,1,0:T(8,128)S(1)} %copy-done.2), kind=kOutput, calls=%fused_computation.8 | convolution fusion | flops 805306368 | bytes 2359296 | tf_op jit(solution)/shard_map/ck,jk->cj/dot_general | solution.py:11
  98.6 0.0 copy-done.1
  98.7 5.7 %bitcast_subtract_fusion.1 = f32[1024,1024]{0,1:T(8,128)S(1)} fusion(f32[1024,1024]{0,1:T(8,128)} %copy.4, f32[1024,256]{1,0:T(8,128)S(1)} %fusion.4, f32[2,1024,256]{1,2,0:T(8,128)S(1)} %copy-done.1), kind=kOutput, calls=%fused_computation.1 | convolution fusion | flops 3222274048 | bytes 10485760 | tf_op jit(solution)/shard_map/rj,cj->rc/dot_general | solution.py:12
  104.4 0.0 copy-start
  104.4 2.0 %copy-done = f32[1024,1024]{0,1:T(8,128)} copy-done((f32[1024,1024]{0,1:T(8,128)}, f32[1024,1024]{0,1:T(8,128)S(1)}, u32[]{:S(2)}) %copy-start) | copy-done | bytes 4194328
  106.4 4.5 %fusion.1 = f32[1024,256]{1,0:T(8,128)} fusion(f32[1024,1024]{0,1:T(8,128)S(1)} %bitcast_subtract_fusion.1, f32[2,1024,256]{1,2,0:T(8,128)S(1)} %copy-done.1), kind=kOutput, calls=%fused_computation.5 | convolution fusion | flops 3221225472 | bytes 6291456 | tf_op jit(solution)/shard_map/rc,rk->ck/dot_general | solution.py:9
  110.9 0.0 all-reduce.5.cloned.1.call-update
  110.9 51.4 %all-reduce.5.cloned.1.call-done = f32[1024,256]{1,0:T(8,128)} async-done(((f32[1024,256]{1,0:T(8,128)}), f32[1024,256]{1,0:T(8,128)}) %all-reduce.5.cloned.1.call-update) | async-done | bytes 1048592 | tf_op jit(solution)/shard_map/psum | solution.py:10
  162.3 2.3 %fusion.2 = f32[1024,256]{1,0:T(8,128)S(1)} fusion(f32[1024,256]{1,0:T(8,128)} %all-reduce.5.cloned.1.call-done, f32[2,256,256]{2,1,0:T(8,128)S(1)} %copy-done.2), kind=kOutput, calls=%fused_computation.6 | convolution fusion | flops 805306368 | bytes 2359296 | tf_op jit(solution)/shard_map/ck,jk->cj/dot_general | solution.py:11
  164.5 6.6 %bitcast_subtract_fusion = f32[1024,1024]{0,1:T(8,128)} fusion(f32[1024,1024]{0,1:T(8,128)} %copy-done, f32[1024,256]{1,0:T(8,128)S(1)} %fusion.2, f32[2,1024,256]{1,2,0:T(8,128)S(1)} %copy-done.1), kind=kOutput, calls=%fused_computation | convolution fusion | flops 3222274048 | bytes 10485760 | tf_op jit(solution)/shard_map/rj,cj->rc/dot_general | solution.py:12
  171.1 5.3 %copy.5 = f32[1024,1024]{1,0:T(8,128)} copy(f32[1024,1024]{0,1:T(8,128)} %bitcast_subtract_fusion) | data formatting | bytes 8388608 | tf_op jit(solution)/shard_map/sub | solution.py:12
Async XLA Ops:
  6.5 27.7 %all-gather.2.cloned.1.call-start = ((), (), s32[]{:S(2)}) async-start(), calls=%async_computation | async-start | bytes 2621440 | tf_op jit(solution)/shard_map/all_gather | solution.py:16
  7.3 89.1 %all-reduce.3.cloned.1.call-start = ((), (), s32[]{:S(2)}) async-start(), calls=%async_computation.1 | async-start | bytes 2097152 | tf_op jit(solution)/shard_map/psum | solution.py:10
  44.4 52.0 %copy-start.2 = (f32[2,256,256]{2,1,0:T(8,128)S(1)}, f32[2,256,256]{2,1,0:T(8,128)}, u32[]{:S(2)}) copy-start(f32[2,256,256]{2,1,0:T(8,128)} %param.5) | copy-start | bytes 1572868
  44.4 54.2 %copy-start.1 = (f32[2,1024,256]{1,2,0:T(8,128)S(1)}, f32[2,1024,256]{1,2,0:T(8,128)}, u32[]{:S(2)}) copy-start(f32[2,1024,256]{1,2,0:T(8,128)} %all-gather.2.cloned.1.call-done) | copy-start | bytes 6291460
  44.4 117.8 %all-reduce.5.cloned.1.call-start = ((), (), s32[]{:S(2)}) async-start(), calls=%async_computation.2 | async-start | bytes 2097152 | tf_op jit(solution)/shard_map/psum | solution.py:10
  104.4 2.0 %copy-start = (f32[1024,1024]{0,1:T(8,128)}, f32[1024,1024]{0,1:T(8,128)S(1)}, u32[]{:S(2)}) copy-start(f32[1024,1024]{0,1:T(8,128)S(1)} %bitcast_subtract_fusion.1) | copy-start | bytes 12582916
Sparse Core Ops, SparseCore 0:
  8.9 25.2 all-gather.1
  44.5 51.8 all-reduce.2
  111.0 51.1 all-reduce.4
where the time goes:
time: 183 us
  waiting for transfers between devices  125 us (68%)
  matrix products  31.4 us (17%)
  between operations  13.2 us (7%)
  local copies, waits for them, and re-layouts  12.8 us (7%)
    psum x2, waiting for transfers between devices, update(): sums = lax.psum(local_sums, 'prow')  97.6 us
    all_gather x1, waiting for transfers between devices, per_device(): gathered = lax.all_gather(y_panels, 'pcol', axis=2, tiled=True)  26.9 us
    dot_general x2, matrix products, update(): local_sums = jnp.einsum('rc,rk->ck', current, vectors, precision=highest)  14.6 us
    dot_general x2, matrix products, update(): return current - jnp.einsum('rj,cj->rc', vectors, scaled, precision=highest)  12.3 us
    unnamed x7, local copies, waits for them, and re-layouts  7.5 us
    sub x1, local copies, waits for them, and re-layouts, update(): return current - jnp.einsum('rj,cj->rc', vectors, scaled, precision=highest)  5.34 us
    dot_general x2, matrix products, update(): scaled = jnp.einsum('ck,jk->cj', sums, triangle, precision=highest)  4.51 us
  transfers between devices with their start and end apart: 3, of which 3 were waited for; matrix products, arithmetic and copies ran while one was open for 3% of the time, Pallas kernels for 0%

commit v1 on v0

v1 whole, which is shorter than its diff:
```python
import functools

import jax
import jax.numpy as jnp
from jax import lax
from jax.experimental import pallas as pl
from jax.experimental.pallas import tpu as pltpu
from jax.sharding import PartitionSpec as P

F32 = jnp.float32
BF16 = jnp.bfloat16
BLOCK = 256
SUBS = 2
MESH = pl.DeviceIdType.MESH


def split(x):
    high = x.astype(BF16)
    return high, (x - high.astype(F32)).astype(BF16)


def dot3(ah, al, bh, bl, dims):
    dot = functools.partial(
        lax.dot_general, dimension_numbers=(dims, ((), ())), preferred_element_type=F32
    )
    return dot(ah, bh) + (dot(al, bh) + dot(ah, bl))


def kernel(
    rows, nprow, npcol,
    v_hbm, y_hbm, t_hbm, out_hbm,
    vbuf, vh, vl, ybuf, yt, yth, ytl, tbuf, zh, zl, sbuf, ab, sth, stl,
    v_sem, y_sem, t_sem, out_sem,
    ys_sem, yx_sem, yf_sem, yr_sem,
    in_send, in_recv, outw_send,
):
    npan = y_hbm.shape[0]
    kc = y_hbm.shape[2]
    ncb = vbuf.shape[0]
    nx = npcol // 2
    per_phase = ncb * nx
    units = npan * per_phase
    piece = 2 * kc // SUBS
    cb = vbuf.shape[2]

    grp = lax.axis_index("grp")
    row = lax.axis_index("prow")
    col = lax.axis_index("pcol")
    x, core = col // 2, col % 2
    half = nprow // 2
    lower = row < half
    inner = jnp.where(lower, row + 1, row - 1)
    outer = jnp.where(lower, row - 1, row + 1)
    dist = jnp.where(lower, half - 1 - row, row - half)
    centre = dist == 0
    edge = dist == half - 1
    centre_slot = jnp.where(centre, 1, 0)
    lag_cap = min(
        [per_phase + j * nx - ((nx - 1) * (ncb - 1) + j) - 1 for j in range(ncb - 1)]
        + [(ncb - 1) * nx]
    )
    lag = jnp.minimum(2 + 2 * dist, lag_cap)
    max_lag = min(2 + 2 * (half - 1), lag_cap)

    sibling = (grp, row, x * 2 + 1 - core)

    def across(g):
        return (grp, row, ((x + g) % nx) * 2 + core)

    def v_load(j):
        start = pl.multiple_of(j * cb, cb)
        return pltpu.make_async_copy(v_hbm.at[:, pl.ds(start, cb)], vbuf.at[j], v_sem.at[j])

    def out_store(j):
        start = pl.multiple_of(j * cb, cb)
        return pltpu.make_async_copy(vbuf.at[j], out_hbm.at[:, pl.ds(start, cb)], out_sem.at[j])

    def y_load(p):
        return pltpu.make_async_copy(y_hbm.at[p], ybuf.at[p], y_sem.at[p])

    t_load = pltpu.make_async_copy(t_hbm, tbuf, t_sem)
    for p in reversed(range(npan)):
        y_load(p).start()
    for j in range(ncb):
        v_load(j).start()
    t_load.start()

    barrier = pltpu.get_barrier_semaphore()
    pl.semaphore_signal(barrier, inc=1, device_id=(grp, inner, col), device_id_type=MESH)

    @pl.when(jnp.logical_not(edge))
    def _():
        pl.semaphore_signal(barrier, inc=1, device_id=(grp, outer, col), device_id_type=MESH)

    pl.semaphore_signal(barrier, inc=1, device_id=sibling, device_id_type=MESH)
    for g in range(1, nx):
        pl.semaphore_signal(barrier, inc=1, device_id=across(g), device_id_type=MESH)

    for p in reversed(range(npan)):
        y_load(p).wait()
        yt[p, x, core] = jnp.transpose(ybuf[p])

    pl.semaphore_wait(barrier, jnp.where(edge, 1, 2) + nx)

    def y_copy(p, chip, which, send_sem, target):
        return pltpu.make_async_remote_copy(
            src_ref=yt.at[p, chip, which],
            dst_ref=yt.at[p, chip, which],
            send_sem=send_sem,
            recv_sem=yr_sem.at[p, chip, which],
            device_id=target,
            device_id_type=MESH,
        )

    def y_sib(p):
        return y_copy(p, x, core, ys_sem.at[p], sibling)

    def y_across(p, g):
        return y_copy(p, x, core, yx_sem.at[p, g - 1], across(g))

    def chip_at(g):
        return (x + g) % nx

    def y_forward(p, g):
        return y_copy(p, chip_at(g), core, yf_sem.at[p, g - 1], sibling)

    def y_arrived(p, chip, which):
        y_copy(p, chip, which, ys_sem.at[p], sibling).wait_recv()

    def split_y(p, chip):
        high, low = split(yt[p, chip].reshape(2 * kc, rows))
        yth[p, chip] = high
        ytl[p, chip] = low

    def forward_all(p):
        for g in range(1, nx):
            y_arrived(p, chip_at(g), core)
            y_forward(p, g).start()

    def finish_panel(p):
        for g in range(1, nx):
            y_arrived(p, chip_at(g), 1 - core)
            split_y(p, chip_at(g))
        th, tl = split(tbuf[p])
        z = dot3(
            yth[p].reshape(2 * kc * nx, rows), ytl[p].reshape(2 * kc * nx, rows),
            th, tl, ((0,), (0,)),
        )
        high, low = split(z)
        zh[p] = high
        zl[p] = low

    for p in reversed(range(npan)):
        y_sib(p).start()
        if p == npan - 1:
            for g in range(1, nx):
                y_across(p, g).start()
    t_load.wait()
    y_arrived(npan - 1, x, 1 - core)
    split_y(npan - 1, x)

    def decode(u):
        phase = u // per_phase
        r = u % per_phase
        last = r >= (ncb - 1) * nx
        first = phase == 0
        j = jnp.where(first, jnp.where(last, ncb - 1, r % (ncb - 1)), r // nx)
        g = jnp.where(first, jnp.where(last, r - (ncb - 1) * nx, r // (ncb - 1)), r % nx)
        return phase, npan - 1 - phase, j, g

    def inward(u, s):
        at = pl.ds(s * piece, piece)
        return pltpu.make_async_remote_copy(
            src_ref=sbuf.at[u, at],
            dst_ref=ab.at[centre_slot, u, at],
            send_sem=in_send.at[u, s],
            recv_sem=in_recv.at[centre_slot, u, s],
            device_id=(grp, inner, col),
            device_id_type=MESH,
        )

    def outward(u, s):
        at = pl.ds(s * piece, piece)
        return pltpu.make_async_remote_copy(
            src_ref=ab.at[1, u, at],
            dst_ref=ab.at[1, u, at],
            send_sem=outw_send.at[u, s],
            recv_sem=in_recv.at[1, u, s],
            device_id=(grp, outer, col),
            device_id_type=MESH,
        )

    def arrived(slot, u, s):
        at = pl.ds(s * piece, piece)
        pltpu.make_async_remote_copy(
            src_ref=sbuf.at[u, at],
            dst_ref=ab.at[slot, u, at],
            send_sem=in_send.at[u, s],
            recv_sem=in_recv.at[slot, u, s],
            device_id=(grp, inner, col),
            device_id_type=MESH,
        ).wait_recv()

    begin = max(ncb - 2, 0)

    def step(t, carry):
        for f in range(npan):
            p = npan - 1 - f
            if f == 0:
                forward_at, finish_at = begin, begin + 1
            else:
                base = (f - 1) * per_phase + begin
                send_at, forward_at, finish_at = base + 1, base + 3, base + 4

                @pl.when(t == send_at)
                def _():
                    for g in range(1, nx):
                        y_across(p, g).start()

            @pl.when(t == forward_at)
            def _():
                forward_all(p)

            @pl.when(t == finish_at)
            def _():
                if f > 0:
                    y_arrived(p, x, 1 - core)
                    split_y(p, x)
                finish_panel(p)

        @pl.when(t < units)
        def _():
            u = t
            phase, p, j, g = decode(u)

            @pl.when(jnp.logical_and(phase == 0, g == 0))
            def _():
                v_load(j).wait()
                high, low = split(vbuf[j])
                vh[j] = high
                vl[j] = low

            chip = chip_at(g)
            sbuf[u] = dot3(yth[p, chip], ytl[p, chip], vh[j], vl[j], ((1,), (0,)))
            for s in range(SUBS):
                at = pl.ds(s * piece, piece)

                @pl.when(jnp.logical_not(edge))
                def _():
                    arrived(0, u, s)
                    sbuf[u, at] = sbuf[u, at] + ab[0, u, at]

                inward(u, s).start()

        w = t - lag

        @pl.when(jnp.logical_and(w >= 0, w < units))
        def _():
            phase, p, j, g = decode(w)
            chip = chip_at(g)
            for s in range(SUBS):
                at = pl.ds(s * piece, piece)
                arrived(1, w, s)

                @pl.when(centre)
                def _():
                    ab[1, w, at] = ab[1, w, at] + sbuf[w, at]

                @pl.when(jnp.logical_not(edge))
                def _():
                    outward(w, s).start()

                high, low = split(ab[1, w, at])
                sth[j, chip, at] = high
                stl[j, chip, at] = low

            @pl.when(g == nx - 1)
            def _():
                bh = sth[j].reshape(2 * kc * nx, cb)
                bl = stl[j].reshape(2 * kc * nx, cb)
                for r in range(0, rows, BLOCK):
                    at = pl.ds(r, BLOCK)
                    new = vbuf[j, at] - dot3(zh[p, at], zl[p, at], bh, bl, ((1,), (0,)))
                    vbuf[j, at] = new

                    @pl.when(phase < npan - 1)
                    def _():
                        high, low = split(vbuf[j, at])
                        vh[j, at] = high
                        vl[j, at] = low

                @pl.when(phase == npan - 1)
                def _():
                    out_store(j).start()

        return carry

    lax.fori_loop(0, units + max_lag, step, 0)

    for p in range(npan):
        y_sib(p).wait_send()
        for g in range(1, nx):
            y_across(p, g).wait_send()
            y_forward(p, g).wait_send()

    def drain(u, carry):
        for s in range(SUBS):
            inward(u, s).wait_send()

            @pl.when(jnp.logical_not(edge))
            def _():
                outward(u, s).wait_send()

        return carry

    lax.fori_loop(0, units, drain, 0)
    for j in range(ncb):
        out_store(j).wait()


def per_device(nprow, npcol, eigvecs, y_panels, t_factors):
    rows, cols = eigvecs.shape
    npan, _, kc = y_panels.shape
    cb = BLOCK
    ncb = cols // cb
    nx = npcol // 2
    units = npan * ncb * nx
    dma = pltpu.SemaphoreType.DMA
    any_space = pl.BlockSpec(memory_space=pl.ANY)
    nb = kc * npcol
    return pl.pallas_call(
        functools.partial(kernel, rows, nprow, npcol),
        out_shape=jax.ShapeDtypeStruct((rows, cols), F32),
        in_specs=[any_space] * 3,
        out_specs=any_space,
        scratch_shapes=[
            pltpu.VMEM((ncb, rows, cb), F32),
            pltpu.VMEM((ncb, rows, cb), BF16),
            pltpu.VMEM((ncb, rows, cb), BF16),
            pltpu.VMEM((npan, rows, kc), F32),
            pltpu.VMEM((npan, nx, 2, kc, rows), F32),
            pltpu.VMEM((npan, nx, 2 * kc, rows), BF16),
            pltpu.VMEM((npan, nx, 2 * kc, rows), BF16),
            pltpu.VMEM((npan, nb, nb), F32),
            pltpu.VMEM((npan, rows, nb), BF16),
            pltpu.VMEM((npan, rows, nb), BF16),
            pltpu.VMEM((units, 2 * kc, cb), F32),
            pltpu.VMEM((2, units, 2 * kc, cb), F32),
            pltpu.VMEM((ncb, nx, 2 * kc, cb), BF16),
            pltpu.VMEM((ncb, nx, 2 * kc, cb), BF16),
            dma((ncb,)),
            dma((npan,)),
            dma,
            dma((ncb,)),
            dma((npan,)),
            dma((npan, nx - 1)),
            dma((npan, nx - 1)),
            dma((npan, nx, 2)),
            dma((units, SUBS)),
            dma((2, units, SUBS)),
            dma((units, SUBS)),
        ],
        compiler_params=pltpu.CompilerParams(
            collective_id=0, has_side_effects=True, vmem_limit_bytes=50 * 2**20
        ),
        cost_estimate=pl.CostEstimate(
            flops=2 * 3 * npan * rows * nb * (2 * cols + nb),
            bytes_accessed=8 * rows * cols,
            transcendentals=0,
        ),
    )(eigvecs, y_panels, t_factors)


def solution(mesh):
    return jax.shard_map(
        functools.partial(per_device, mesh.shape["prow"], mesh.shape["pcol"]),
        mesh=mesh,
        in_specs=(
            P(("grp", "prow"), "pcol"),
            P(None, ("grp", "prow"), "pcol"),
            P("grp", None, None),
        ),
        out_specs=P(("grp", "prow"), "pcol"),
        check_vma=False,
    )
```

time: 183 us -> 82.9 us (0.45)
  waiting for transfers between devices: 125 us -> 0 us
  Pallas kernels: 0 us -> 75.4 us
  matrix products: 31.4 us -> 0 us
  between operations: 13.2 us -> 0.03 us
  local copies, waits for them, and re-layouts: 12.8 us -> 7.2 us
    psum x2 -> x0, waiting for transfers between devices: 97.6 us -> none  [update(): sums = lax.psum(local_sums, 'prow')]
    pallas_call x0 -> x1, Pallas kernels: none -> 75.4 us  [per_device(): pl.pallas_call(functools.partial(kernel, rows, nprow, npcol), out_shape=j...]
    dot_general x6 -> x0, matrix products: 31.4 us -> none  [the longest x2 14.6 us: update(): local_sums = jnp.einsum('rc,rk->ck', current, vectors, precision=highest)]
    all_gather x1 -> x0, waiting for transfers between devices: 26.9 us -> none  [per_device(): gathered = lax.all_gather(y_panels, 'pcol', axis=2, tiled=True)]
    sub x1 -> x0, local copies, waits for them, and re-layouts: 5.34 us -> none  [update(): return current - jnp.einsum('rj,cj->rc', vectors, scaled, precision=highest)]
    unnamed x7 -> x4, local copies, waits for them, and re-layouts: 7.5 us -> 7.2 us
  transfers between devices with their start and end apart: 3 -> 0, of which waited for: 3 -> 0; matrix products, arithmetic and copies ran while one was open for 3% -> 0% of each run, Pallas kernels for 0% -> 0%
where the time goes in v1:
time: 82.9 us; the launch traced here: 82.6 us
  Pallas kernels  75.4 us (91%)
  local copies, waits for them, and re-layouts  7.2 us (9%)
    pallas_call x1, Pallas kernels, per_device(): pl.pallas_call(functools.partial(kernel, rows, nprow, npcol), out_shape=j...  75.4 us
    unnamed x4, local copies, waits for them, and re-layouts  7.2 us

profile of v1, /device:TPU:0, one launch (start us, length us, event | category | flops | bytes accessed | tf_op | source)
XLA Modules:
  0.0 82.6 jit_solution(2224106008070000889)
XLA Ops:
  0.0 1.4 %copy.4.y_hbm = f32[2,1024,64]{2,1,0:T(8,128)S(1)} copy(f32[2,1024,64]{1,2,0:T(8,128)} %param.4) | data formatting | bytes 1048576 | tf_op args[1]
  1.4 0.0 copy-start
  1.4 1.0 %copy-done = f32[2,256,256]{2,1,0:T(8,128)S(1)} copy-done((f32[2,256,256]{2,1,0:T(8,128)S(1)}, f32[2,256,256]{2,1,0:T(8,128)}, u32[]{:S(2)}) %copy-start) | copy-done | bytes 524312
  2.4 75.4 %shard_map.37 = f32[1024,1024]{1,0:T(8,128)} custom-call(f32[1024,1024]{1,0:T(8,128)} %v_hbm.1, f32[2,1024,64]{2,1,0:T(8,128)S(1)} %copy.4.y_hbm, f32[2,256,256]{2,1,0:T(8,128)S(1)} %copy-done), custom_call_target="tpu_custom_call" | custom-call | flops 7247757312 | bytes 8388608 | tf_op jit(solution)/shard_map/pallas_call | solution.py:331
  77.9 4.8 %copy.6 = f32[1024,1024]{1,0:T(8,128)} copy(f32[1024,1024]{1,0:T(8,128)} %shard_map.37) | data formatting | bytes 8388608
Async XLA Ops:
  1.4 1.0 %copy-start = (f32[2,256,256]{2,1,0:T(8,128)S(1)}, f32[2,256,256]{2,1,0:T(8,128)}, u32[]{:S(2)}) copy-start(f32[2,256,256]{2,1,0:T(8,128)} %t_hbm.1) | copy-start | bytes 1572868

commit v2 on v1

--- a/solution.py
+++ b/solution.py
@@ -11,6 +11,7 @@
 BF16 = jnp.bfloat16
 BLOCK = 256
 SUBS = 2
+LAG = 1
 MESH = pl.DeviceIdType.MESH
 
 
@@ -28,14 +29,14 @@
 
 def kernel(
     rows, nprow, npcol,
-    v_hbm, y_hbm, t_hbm, out_hbm,
-    vbuf, vh, vl, ybuf, yt, yth, ytl, tbuf, zh, zl, sbuf, ab, sth, stl,
-    v_sem, y_sem, t_sem, out_sem,
+    v_hbm, y_hbm, t_hbm, out,
+    vbuf, vh, vl, yt, yth, ytl, tbuf, zh, zl, sbuf, ab, sth, stl,
+    v_sem, y_sem, t_sem,
     ys_sem, yx_sem, yf_sem, yr_sem,
     in_send, in_recv, outw_send,
 ):
     npan = y_hbm.shape[0]
-    kc = y_hbm.shape[2]
+    kc = y_hbm.shape[1]
     ncb = vbuf.shape[0]
     nx = npcol // 2
     per_phase = ncb * nx
@@ -59,8 +60,8 @@
         [per_phase + j * nx - ((nx - 1) * (ncb - 1) + j) - 1 for j in range(ncb - 1)]
         + [(ncb - 1) * nx]
     )
-    lag = jnp.minimum(2 + 2 * dist, lag_cap)
-    max_lag = min(2 + 2 * (half - 1), lag_cap)
+    lag = jnp.minimum(LAG + 3 * dist, lag_cap)
+    max_lag = min(LAG + 3 * (half - 1), lag_cap)
 
     sibling = (grp, row, x * 2 + 1 - core)
 
@@ -71,12 +72,8 @@
         start = pl.multiple_of(j * cb, cb)
         return pltpu.make_async_copy(v_hbm.at[:, pl.ds(start, cb)], vbuf.at[j], v_sem.at[j])
 
-    def out_store(j):
-        start = pl.multiple_of(j * cb, cb)
-        return pltpu.make_async_copy(vbuf.at[j], out_hbm.at[:, pl.ds(start, cb)], out_sem.at[j])
-
     def y_load(p):
-        return pltpu.make_async_copy(y_hbm.at[p], ybuf.at[p], y_sem.at[p])
+        return pltpu.make_async_copy(y_hbm.at[p], yt.at[p, x, core], y_sem.at[p])
 
     t_load = pltpu.make_async_copy(t_hbm, tbuf, t_sem)
     for p in reversed(range(npan)):
@@ -98,8 +95,6 @@
 
     for p in reversed(range(npan)):
         y_load(p).wait()
-        yt[p, x, core] = jnp.transpose(ybuf[p])
-
     pl.semaphore_wait(barrier, jnp.where(edge, 1, 2) + nx)
 
     def y_copy(p, chip, which, send_sem, target):
@@ -128,9 +123,13 @@
         y_copy(p, chip, which, ys_sem.at[p], sibling).wait_recv()
 
     def split_y(p, chip):
-        high, low = split(yt[p, chip].reshape(2 * kc, rows))
-        yth[p, chip] = high
-        ytl[p, chip] = low
+        for which in range(2):
+            split_half(p, chip, which)
+
+    def split_half(p, chip, which):
+        high, low = split(yt[p, chip, which])
+        yth[p, chip, which] = high
+        ytl[p, chip, which] = low
 
     def forward_all(p):
         for g in range(1, nx):
@@ -141,6 +140,8 @@
         for g in range(1, nx):
             y_arrived(p, chip_at(g), 1 - core)
             split_y(p, chip_at(g))
+
+    def factor_panel(p):
         th, tl = split(tbuf[p])
         z = dot3(
             yth[p].reshape(2 * kc * nx, rows), ytl[p].reshape(2 * kc * nx, rows),
@@ -155,9 +156,7 @@
         if p == npan - 1:
             for g in range(1, nx):
                 y_across(p, g).start()
-    t_load.wait()
-    y_arrived(npan - 1, x, 1 - core)
-    split_y(npan - 1, x)
+    split_half(npan - 1, x, core)
 
     def decode(u):
         phase = u // per_phase
@@ -201,26 +200,32 @@
             device_id_type=MESH,
         ).wait_recv()
 
+    def pass_inward(u, s):
+        at = pl.ds(pl.multiple_of(s * piece, piece), piece)
+
+        @pl.when(jnp.logical_not(edge))
+        def _():
+            arrived(0, u, s)
+            sbuf[u, at] = sbuf[u, at] + ab[0, u, at]
+
+        inward(u, s).start()
+
     begin = max(ncb - 2, 0)
 
     def step(t, carry):
         for f in range(npan):
             p = npan - 1 - f
             if f == 0:
-                forward_at, finish_at = begin, begin + 1
+                finish_at = begin + 1
             else:
                 base = (f - 1) * per_phase + begin
-                send_at, forward_at, finish_at = base + 1, base + 3, base + 4
+                send_at, finish_at = base + 1, base + 4
 
                 @pl.when(t == send_at)
                 def _():
                     for g in range(1, nx):
                         y_across(p, g).start()
 
-            @pl.when(t == forward_at)
-            def _():
-                forward_all(p)
-
             @pl.when(t == finish_at)
             def _():
                 if f > 0:
@@ -241,16 +246,39 @@
                 vl[j] = low
 
             chip = chip_at(g)
-            sbuf[u] = dot3(yth[p, chip], ytl[p, chip], vh[j], vl[j], ((1,), (0,)))
-            for s in range(SUBS):
-                at = pl.ds(s * piece, piece)
-
-                @pl.when(jnp.logical_not(edge))
-                def _():
-                    arrived(0, u, s)
-                    sbuf[u, at] = sbuf[u, at] + ab[0, u, at]
-
-                inward(u, s).start()
+
+            @pl.when(t == 0)
+            def _():
+                for turn, which in enumerate((core, 1 - core)):
+                    if turn == 1:
+                        y_arrived(p, x, which)
+                        split_half(p, x, which)
+                    sbuf[u, pl.ds(which * kc, kc)] = dot3(
+                        yth[p, chip, which], ytl[p, chip, which], vh[j], vl[j], ((1,), (0,))
+                    )
+                    pass_inward(u, which)
+
+            @pl.when(t > 0)
+            def _():
+                sbuf[u] = dot3(
+                    yth[p, chip].reshape(2 * kc, rows), ytl[p, chip].reshape(2 * kc, rows),
+                    vh[j], vl[j], ((1,), (0,)),
+                )
+                for s in range(SUBS):
+                    pass_inward(u, s)
+
+        for f in range(npan):
+            base = max(f - 1, 0) * per_phase + begin
+
+            @pl.when(t == base + (0 if f == 0 else 3))
+            def _():
+                forward_all(npan - 1 - f)
+
+            @pl.when(t == base + (1 if f == 0 else 4))
+            def _():
+                if f == 0:
+                    t_load.wait()
+                factor_panel(npan - 1 - f)
 
         w = t - lag
 
@@ -289,9 +317,9 @@
                         vh[j, at] = high
                         vl[j, at] = low
 
-                @pl.when(phase == npan - 1)
-                def _():
-                    out_store(j).start()
+                    @pl.when(phase == npan - 1)
+                    def _():
+                        out[at, pl.ds(pl.multiple_of(j * cb, cb), cb)] = vbuf[j, at]
 
         return carry
 
@@ -314,8 +342,6 @@
         return carry
 
     lax.fori_loop(0, units, drain, 0)
-    for j in range(ncb):
-        out_store(j).wait()
 
 
 def per_device(nprow, npcol, eigvecs, y_panels, t_factors):
@@ -326,21 +352,20 @@
     nx = npcol // 2
     units = npan * ncb * nx
     dma = pltpu.SemaphoreType.DMA
-    any_space = pl.BlockSpec(memory_space=pl.ANY)
+    any_space = pl.BlockSpec(memory_space=pltpu.HBM)
     nb = kc * npcol
     return pl.pallas_call(
         functools.partial(kernel, rows, nprow, npcol),
         out_shape=jax.ShapeDtypeStruct((rows, cols), F32),
         in_specs=[any_space] * 3,
-        out_specs=any_space,
+        out_specs=pl.BlockSpec(memory_space=pltpu.VMEM),
         scratch_shapes=[
             pltpu.VMEM((ncb, rows, cb), F32),
             pltpu.VMEM((ncb, rows, cb), BF16),
             pltpu.VMEM((ncb, rows, cb), BF16),
-            pltpu.VMEM((npan, rows, kc), F32),
             pltpu.VMEM((npan, nx, 2, kc, rows), F32),
-            pltpu.VMEM((npan, nx, 2 * kc, rows), BF16),
-            pltpu.VMEM((npan, nx, 2 * kc, rows), BF16),
+            pltpu.VMEM((npan, nx, 2, kc, rows), BF16),
+            pltpu.VMEM((npan, nx, 2, kc, rows), BF16),
             pltpu.VMEM((npan, nb, nb), F32),
             pltpu.VMEM((npan, rows, nb), BF16),
             pltpu.VMEM((npan, rows, nb), BF16),
@@ -351,7 +376,6 @@
             dma((ncb,)),
             dma((npan,)),
             dma,
-            dma((ncb,)),
             dma((npan,)),
             dma((npan, nx - 1)),
             dma((npan, nx - 1)),
@@ -361,14 +385,18 @@
             dma((units, SUBS)),
         ],
         compiler_params=pltpu.CompilerParams(
-            collective_id=0, has_side_effects=True, vmem_limit_bytes=50 * 2**20
+            collective_id=0, has_side_effects=True, vmem_limit_bytes=48 * 2**20
         ),
         cost_estimate=pl.CostEstimate(
             flops=2 * 3 * npan * rows * nb * (2 * cols + nb),
             bytes_accessed=8 * rows * cols,
             transcendentals=0,
         ),
-    )(eigvecs, y_panels, t_factors)
+    )(
+        eigvecs,
+        pltpu.with_memory_space_constraint(jnp.swapaxes(y_panels, 1, 2), pltpu.HBM),
+        pltpu.with_memory_space_constraint(t_factors, pltpu.HBM),
+    )
 
 
 def solution(mesh):

time: 82.9 us -> 69.6 us (0.84)
  Pallas kernels: 75.4 us -> 67.4 us
  local copies, waits for them, and re-layouts: 7.2 us -> 2.02 us
    pallas_call x1, Pallas kernels: 75.4 us -> 67.4 us  [per_device(): pl.pallas_call(functools.partial(kernel, rows, nprow, npcol), out_shape=j...]
    unnamed x4 -> x1, local copies, waits for them, and re-layouts: 7.2 us -> 2.02 us
where the time goes in v2:
time: 69.6 us; the launch traced here: 69.4 us
  Pallas kernels  67.4 us (97%)
  local copies, waits for them, and re-layouts  2.02 us (3%)
    pallas_call x1, Pallas kernels, per_device(): pl.pallas_call(functools.partial(kernel, rows, nprow, npcol), out_shape=j...  67.4 us
    unnamed x1, local copies, waits for them, and re-layouts  2.02 us

profile of v2, /device:TPU:0, one launch (start us, length us, event | category | flops | bytes accessed | tf_op | source)
XLA Modules:
  0.0 69.4 jit_solution(5279459764337909347)
XLA Ops:
  0.0 67.4 %shard_map.37 = f32[1024,1024]{1,0:T(8,128)S(1)} custom-call(f32[1024,1024]{1,0:T(8,128)} %v_hbm.1, f32[2,64,1024]{2,1,0:T(8,128)} %bitcast.1, f32[2,256,256]{2,1,0:T(8,128)} %t_hbm.1), custom_call_target="tpu_custom_call" | custom-call | flops 7247757312 | bytes 8388608 | tf_op jit(solution)/shard_map/pallas_call | solution.py:357
  67.4 2.0 %copy.5 = f32[1024,1024]{1,0:T(8,128)} copy(f32[1024,1024]{1,0:T(8,128)S(1)} %shard_map.37) | data formatting | bytes 8388608

commit v3 on v2

--- a/solution.py
+++ b/solution.py
@@ -30,7 +30,7 @@
 def kernel(
     rows, nprow, npcol,
     v_hbm, y_hbm, t_hbm, out,
-    vbuf, vh, vl, yt, yth, ytl, tbuf, zh, zl, sbuf, ab, sth, stl,
+    vbuf, vh, vl, yt, yth, ytl, tbuf, z3, sbuf, ab, st3,
     v_sem, y_sem, t_sem,
     ys_sem, yx_sem, yf_sem, yr_sem,
     in_send, in_recv, outw_send,
@@ -39,6 +39,7 @@
     kc = y_hbm.shape[1]
     ncb = vbuf.shape[0]
     nx = npcol // 2
+    nb = kc * npcol
     per_phase = ncb * nx
     units = npan * per_phase
     piece = 2 * kc // SUBS
@@ -61,6 +62,7 @@
         + [(ncb - 1) * nx]
     )
     lag = jnp.minimum(LAG + 3 * dist, lag_cap)
+    late = jnp.where(lag < lag_cap, 1, 0)
     max_lag = min(LAG + 3 * (half - 1), lag_cap)
 
     sibling = (grp, row, x * 2 + 1 - core)
@@ -148,8 +150,8 @@
             th, tl, ((0,), (0,)),
         )
         high, low = split(z)
-        zh[p] = high
-        zl[p] = low
+        for part, value in enumerate((high, low, high)):
+            z3[p, :, pl.ds(part * nb, nb)] = value
 
     for p in reversed(range(npan)):
         y_sib(p).start()
@@ -212,6 +214,28 @@
 
     begin = max(ncb - 2, 0)
 
+    def update(w):
+        phase, p, j, g = decode(w)
+
+        @pl.when(g == nx - 1)
+        def _():
+            for r in range(0, rows, rows):
+                at = pl.ds(r, rows)
+                new = vbuf[j, at] - jnp.dot(
+                        z3[p, at], st3[j].reshape(3 * nb, cb), preferred_element_type=F32
+                    )
+                vbuf[j, at] = new
+
+                @pl.when(phase < npan - 1)
+                def _():
+                    high, low = split(vbuf[j, at])
+                    vh[j, at] = high
+                    vl[j, at] = low
+
+                @pl.when(phase == npan - 1)
+                def _():
+                    out[at, pl.ds(pl.multiple_of(j * cb, cb), cb)] = vbuf[j, at]
+
     def step(t, carry):
         for f in range(npan):
             p = npan - 1 - f
@@ -280,6 +304,12 @@
                     t_load.wait()
                 factor_panel(npan - 1 - f)
 
+        before = t - lag - 1
+
+        @pl.when(jnp.logical_and(late == 1, jnp.logical_and(before >= 0, before < units)))
+        def _():
+            update(before)
+
         w = t - lag
 
         @pl.when(jnp.logical_and(w >= 0, w < units))
@@ -299,31 +329,16 @@
                     outward(w, s).start()
 
                 high, low = split(ab[1, w, at])
-                sth[j, chip, at] = high
-                stl[j, chip, at] = low
-
-            @pl.when(g == nx - 1)
-            def _():
-                bh = sth[j].reshape(2 * kc * nx, cb)
-                bl = stl[j].reshape(2 * kc * nx, cb)
-                for r in range(0, rows, BLOCK):
-                    at = pl.ds(r, BLOCK)
-                    new = vbuf[j, at] - dot3(zh[p, at], zl[p, at], bh, bl, ((1,), (0,)))
-                    vbuf[j, at] = new
-
-                    @pl.when(phase < npan - 1)
-                    def _():
-                        high, low = split(vbuf[j, at])
-                        vh[j, at] = high
-                        vl[j, at] = low
-
-                    @pl.when(phase == npan - 1)
-                    def _():
-                        out[at, pl.ds(pl.multiple_of(j * cb, cb), cb)] = vbuf[j, at]
+                for part, value in enumerate((high, high, low)):
+                    st3[j, part, chip, at] = value
+
+        @pl.when(jnp.logical_and(late == 0, jnp.logical_and(w >= 0, w < units)))
+        def _():
+            update(w)
 
         return carry
 
-    lax.fori_loop(0, units + max_lag, step, 0)
+    lax.fori_loop(0, units + max_lag + 1, step, 0)
 
     for p in range(npan):
         y_sib(p).wait_send()
@@ -367,12 +382,10 @@
             pltpu.VMEM((npan, nx, 2, kc, rows), BF16),
             pltpu.VMEM((npan, nx, 2, kc, rows), BF16),
             pltpu.VMEM((npan, nb, nb), F32),
-            pltpu.VMEM((npan, rows, nb), BF16),
-            pltpu.VMEM((npan, rows, nb), BF16),
+            pltpu.VMEM((npan, rows, 3 * nb), BF16),
             pltpu.VMEM((units, 2 * kc, cb), F32),
             pltpu.VMEM((2, units, 2 * kc, cb), F32),
-            pltpu.VMEM((ncb, nx, 2 * kc, cb), BF16),
-            pltpu.VMEM((ncb, nx, 2 * kc, cb), BF16),
+            pltpu.VMEM((ncb, 3, nx, 2 * kc, cb), BF16),
             dma((ncb,)),
             dma((npan,)),
             dma,

time: 69.6 us -> 66.1 us (0.950)
  Pallas kernels: 67.4 us -> 64 us
    pallas_call x1, Pallas kernels: 67.4 us -> 64 us  [per_device(): pl.pallas_call(functools.partial(kernel, rows, nprow, npcol), out_shape=j...]
where the time goes in v3:
time: 66.1 us; the launch traced here: 66 us
  Pallas kernels  64 us (97%)
  local copies, waits for them, and re-layouts  2.02 us (3%)
    pallas_call x1, Pallas kernels, per_device(): pl.pallas_call(functools.partial(kernel, rows, nprow, npcol), out_shape=j...  64 us
    unnamed x1, local copies, waits for them, and re-layouts  2.02 us

profile of v3, /device:TPU:0, one launch (start us, length us, event | category | flops | bytes accessed | tf_op | source)
XLA Modules:
  0.0 66.0 jit_solution(12888964945085233714)
XLA Ops:
  0.0 64.0 %shard_map.37 = f32[1024,1024]{1,0:T(8,128)S(1)} custom-call(f32[1024,1024]{1,0:T(8,128)} %v_hbm.1, f32[2,64,1024]{2,1,0:T(8,128)} %bitcast.1, f32[2,256,256]{2,1,0:T(8,128)} %t_hbm.1), custom_call_target="tpu_custom_call" | custom-call | flops 7247757312 | bytes 8388608 | tf_op jit(solution)/shard_map/pallas_call | solution.py:372
  64.0 2.0 %copy.5 = f32[1024,1024]{1,0:T(8,128)} copy(f32[1024,1024]{1,0:T(8,128)S(1)} %shard_map.37) | data formatting | bytes 8388608

commit v4 on v3

--- a/solution.py
+++ b/solution.py
@@ -219,22 +219,22 @@
 
         @pl.when(g == nx - 1)
         def _():
-            for r in range(0, rows, rows):
-                at = pl.ds(r, rows)
-                new = vbuf[j, at] - jnp.dot(
-                        z3[p, at], st3[j].reshape(3 * nb, cb), preferred_element_type=F32
-                    )
-                vbuf[j, at] = new
-
-                @pl.when(phase < npan - 1)
-                def _():
-                    high, low = split(vbuf[j, at])
-                    vh[j, at] = high
-                    vl[j, at] = low
-
-                @pl.when(phase == npan - 1)
-                def _():
-                    out[at, pl.ds(pl.multiple_of(j * cb, cb), cb)] = vbuf[j, at]
+            def updated():
+                return vbuf[j] - jnp.dot(
+                    z3[p], st3[j].reshape(3 * nb, cb), preferred_element_type=F32
+                )
+
+            @pl.when(phase < npan - 1)
+            def _():
+                new = updated()
+                vbuf[j] = new
+                high, low = split(new)
+                vh[j] = high
+                vl[j] = low
+
+            @pl.when(phase == npan - 1)
+            def _():
+                out[:, pl.ds(pl.multiple_of(j * cb, cb), cb)] = updated()
 
     def step(t, carry):
         for f in range(npan):

time: 66.1 us -> 66.1 us (level)
  no operation moved by 1% of the time
where the time goes in v4:
time: 66.1 us; the launch traced here: 65.9 us
  Pallas kernels  63.9 us (97%)
  local copies, waits for them, and re-layouts  2.02 us (3%)
    pallas_call x1, Pallas kernels, per_device(): pl.pallas_call(functools.partial(kernel, rows, nprow, npcol), out_shape=j...  63.9 us
    unnamed x1, local copies, waits for them, and re-layouts  2.02 us

profile of v4, /device:TPU:0, one launch (start us, length us, event | category | flops | bytes accessed | tf_op | source)
XLA Modules:
  0.0 65.9 jit_solution(13749658742922341922)
XLA Ops:
  0.0 63.9 %shard_map.37 = f32[1024,1024]{1,0:T(8,128)S(1)} custom-call(f32[1024,1024]{1,0:T(8,128)} %v_hbm.1, f32[2,64,1024]{2,1,0:T(8,128)} %bitcast.1, f32[2,256,256]{2,1,0:T(8,128)} %t_hbm.1), custom_call_target="tpu_custom_call" | custom-call | flops 7247757312 | bytes 8388608 | tf_op jit(solution)/shard_map/pallas_call | solution.py:372
  63.9 2.0 %copy.5 = f32[1024,1024]{1,0:T(8,128)} copy(f32[1024,1024]{1,0:T(8,128)S(1)} %shard_map.37) | data formatting | bytes 8388608
